TPU v7x, 256 devices: a whole 4x4x8 slice. The times are simulated.
256 devices in a mesh: seq: 128 (over x, y, z_lo, core), kvh: 2 (over z_hi).
Axes of the slice: x: 4, y: 4, z: 8 (z_hi: 2, z_lo: 4; z = z_hi * 4 + z_lo), core: 2. Of those that a mesh axis runs over, the one named last changes fastest.
Arguments:
- queries: bfloat16 [128, 3, 4, 8, 128], P('seq', None, 'kvh'), may hold values from -125 to 125
- root_kv: bfloat16 [2, 32768, 4, 128], P(None, 'seq', 'kvh'), may hold values from -5 to 5
- doc_kv: bfloat16 [2, 32768, 4, 128], P(None, 'seq', 'kvh'), may hold values from -5 to 5
- suffix_kv: bfloat16 [2, 128, 2048, 4, 128], P(None, 'seq', None, 'kvh'), may hold values from -5 to 5
- new_kv: bfloat16 [2, 128, 3, 4, 128], P(None, 'seq', None, 'kvh'), may hold values from -5 to 5
- suffix_len: int32 [128], P('seq'), may hold values from 1 to 2048, as said below
- request_doc: int32 [128, 1], replicated, may hold values from 0 to 63; in each aligned block of 128 rows (0 to 127, 128 to 255, ...) at most 6 rows name the same one
- owner_list: int32 [128], replicated, may hold values from 0 to 127, each once
- doc_run: int32 [64], replicated, may hold values from 0 to 63, each once
Outputs:
- attended: bfloat16 [128, 3, 4096], P('seq', None, 'kvh')
Inputs may be any that keep to these rules, and one draw needn't show every extreme that they name: `request_doc`: no document is the document of more than 6 requests; some document has exactly 6. `owner_list`: each request id stands in exactly one slot. `doc_run`: each run holds exactly one document. `suffix_len`: some slot has all 2048 suffix slots live.
All inputs are finite; a program needn't handle non-finite values.
Results may differ from a plain program's by a relative error of at most 0.007.
Values may be sent and summed in bfloat16 or wider, within the bound.
A program may use at most 64 MiB of HBM per device.

v0:
```python
import math

import jax
import jax.numpy as jnp
from jax import lax
from jax.sharding import PartitionSpec as P

DOC_LEN = 512


masked_score = -1e30


def scores_of(query_rows, keys):
    return jnp.einsum(
        "btkgd,nkd->btkgn", query_rows, keys, preferred_element_type=jnp.float32
    ) * query_rows.shape[-1] ** (-0.5)


def weights_of(scores, row_top):
    return jnp.exp(scores - row_top[..., None]).astype(jnp.bfloat16)


def weighted(weights, values):
    return jnp.einsum("btkgn,nkd->btkgd", weights, values, preferred_element_type=jnp.float32)


def body(queries, root_kv, doc_kv, suffix_kv, new_kv, suffix_len, request_doc, owner_list, doc_run):
    own_slots = queries.shape[0]
    position = lax.axis_index("seq")
    first_slot = position * own_slots
    everyone = lax.all_gather(queries, "seq", axis=0, tiled=True)
    slot_total = everyone.shape[0]
    slot_run = doc_run[request_doc[owner_list, 0]]
    root_pool, doc_pool = (root_kv, doc_kv)
    group_size = 1
    residue = position % group_size
    group_base = position - residue
    root_keys, root_values = (root_pool[0], root_pool[1])
    doc_keys, doc_values = (doc_pool[0], doc_pool[1])
    doc_width = doc_kv.shape[1]
    row_run = (group_base * doc_width + jnp.arange(doc_pool.shape[1], dtype=jnp.int32)) // DOC_LEN
    doc_match = slot_run[:, None] == row_run[None, :]
    block_size = math.gcd(slot_total, 32)
    block_count = slot_total // block_size
    grouped = everyone.reshape((block_count, block_size) + everyone.shape[1:])
    grouped_match = doc_match.reshape(block_count, block_size, doc_match.shape[1])
    tail_keys = jnp.concatenate([suffix_kv[0], new_kv[0]], 1)
    tail_values = jnp.concatenate([suffix_kv[1], new_kv[1]], 1)
    suffix_span = suffix_kv.shape[2]
    positions = jnp.arange(tail_keys.shape[1], dtype=jnp.int32)
    step_ids = jnp.arange(queries.shape[1], dtype=jnp.int32)
    allowed = jnp.where(
        positions[None, None, :] < suffix_span,
        positions[None, None, :] < suffix_len[:, None, None],
        positions[None, None, :] - suffix_span <= step_ids[None, :, None],
    )
    tail_scores = jnp.einsum(
        "rtkgd,rnkd->rtkgn", queries, tail_keys, preferred_element_type=jnp.float32
    ) * queries.shape[-1] ** (-0.5)
    tail_scores = jnp.where(allowed[:, :, None, None, :], tail_scores, masked_score)

    def doc_masked(query_rows, chosen):
        return jnp.where(
            chosen[:, None, None, None, :], scores_of(query_rows, doc_keys), masked_score
        )

    def root_terms(query_rows, row_top):
        weights = weights_of(scores_of(query_rows, root_keys), row_top)
        return (weighted(weights, root_values), jnp.sum(weights.astype(jnp.float32), -1))

    def block_max(inputs):
        return jnp.maximum(
            jnp.max(scores_of(inputs[0], root_keys), -1),
            jnp.max(doc_masked(inputs[0], inputs[1]), -1),
        )

    maxima = lax.map(block_max, (grouped, grouped_match)).reshape(everyone.shape[:-1])
    all_heads = maxima
    current = lax.dynamic_slice_in_dim(all_heads, first_slot, own_slots, 0)
    all_heads = lax.dynamic_update_slice_in_dim(
        all_heads, jnp.maximum(current, jnp.max(tail_scores, -1)), first_slot, 0
    )
    row_max = lax.pmax(all_heads, "seq")
    grouped_top = row_max.reshape((block_count, block_size) + row_max.shape[1:])

    def block_terms(inputs):
        root_part, root_total = root_terms(inputs[0], inputs[2])
        doc_weights = weights_of(doc_masked(inputs[0], inputs[1]), inputs[2])
        return (
            root_part + weighted(doc_weights, doc_values),
            root_total + jnp.sum(doc_weights.astype(jnp.float32), -1),
        )

    numerator, denominator = lax.map(block_terms, (grouped, grouped_match, grouped_top))
    numerator = numerator.reshape(everyone.shape)
    denominator = denominator.reshape(everyone.shape[:-1])
    full_numerator, full_denominator = lax.psum((numerator, denominator), "seq")
    own_numerator = lax.dynamic_slice_in_dim(full_numerator, first_slot, own_slots, 0)
    own_denominator = lax.dynamic_slice_in_dim(full_denominator, first_slot, own_slots, 0)
    own_top = lax.dynamic_slice_in_dim(row_max, first_slot, own_slots, 0)
    tail_weights = weights_of(tail_scores, own_top)
    own_numerator = own_numerator + jnp.einsum(
        "rtkgn,rnkd->rtkgd", tail_weights, tail_values, preferred_element_type=jnp.float32
    )
    own_denominator = own_denominator + jnp.sum(tail_weights.astype(jnp.float32), -1)
    result = (own_numerator / own_denominator[..., None]).astype(jnp.bfloat16)
    return result.reshape(own_slots, queries.shape[1], -1)


def solution(mesh):
    in_specs = (
        P("seq", None, "kvh", None, None),
        P(None, "seq", "kvh", None),
        P(None, "seq", "kvh", None),
        P(None, "seq", None, "kvh", None),
        P(None, "seq", None, "kvh", None),
        P("seq"),
        P(),
        P(),
        P(),
    )
    out_specs = P("seq", None, "kvh")
    return jax.shard_map(body, mesh=mesh, in_specs=in_specs, out_specs=out_specs, check_vma=False)
```

profile of v0, /device:TPU:1, one launch (start us, length us, event | category | flops | bytes accessed | tf_op | source)
XLA Modules:
  0.0 2222.9 jit_solution(5318233203042781588)
XLA Ops:
  10.6 1.6 gather_fusion.1
  12.3 2.7 fusion.43
  17.6 191.5 %all-gather.2.cloned.1.call-done = bf16[128,3,2,8,128]{4,3,2,1,0:T(8,128)(2,1)} async-done(((bf16[1,3,2,8,128]{4,3,2,1,0:T(8,128)(2,1)}), bf16[128,3,2,8,128]{4,3,2,1,0:T(8,128)(2,1)}) %all-gather.2.cloned.1.call-update) | async-done | bytes 1572880 | tf_op jit(solution)/shard_map/all_gather | solution.py:32
  209.1 2.8 copy.53
  212.0 12.7 while.22
  212.1 1.5 select_reduce_fusion.2
  213.6 1.5 multiply_reduce_fusion.2
  215.2 1.5 select_reduce_fusion.2
  218.4 1.5 select_reduce_fusion.2
  219.9 1.5 multiply_reduce_fusion.2
  221.5 1.5 select_reduce_fusion.2
  223.0 1.5 multiply_reduce_fusion.2
  224.7 659.2 %pmax.7 = f32[128,3,2,8]{3,2,1,0:T(2,128)S(1)} all-reduce(f32[128,3,2,8]{3,2,1,0:T(2,128)S(1)} %fusion.37), channel_id=1, replica_groups=mesh['seq'=128,'kvh'=2] {'seq'}, use_global_device_ids=true, to_apply=%region_5.6 | all-reduce | flops 6144 | bytes 49152 | tf_op jit(solution)/shard_map/pmax | solution.py:84
  884.0 21.5 while.23
  884.1 1.8 convert_reduce_fusion.6
  885.9 1.7 convert_reduce_fusion.5
  889.4 1.8 convert_reduce_fusion.6
  891.2 1.7 convert_reduce_fusion.5
  894.8 1.7 convert_reduce_fusion.6
  896.6 1.7 convert_reduce_fusion.5
  900.2 1.7 convert_reduce_fusion.6
  901.9 1.7 convert_reduce_fusion.5
  905.7 664.3 %psum.15 = f32[128,3,2,8]{3,2,1,0:T(2,128)S(1)} all-reduce(f32[128,3,2,8]{3,2,1,0:T(2,128)S(1)} %bitcast.204), channel_id=1, replica_groups=mesh['seq'=128,'kvh'=2] {'seq'}, use_global_device_ids=true, to_apply=%region_11.12 | all-reduce | flops 6144 | bytes 49152 | tf_op jit(solution)/shard_map/psum | solution.py:98
  1571.2 642.9 %all-reduce.3.cloned.1.call-done = f32[128,3,2,8,128]{4,3,1,2,0:T(8,128)} async-done(((f32[128,3,2,8,128]{4,3,1,2,0:T(8,128)}), f32[128,3,2,8,128]{4,3,1,2,0:T(8,128)}) %all-reduce.3.cloned.1.call-update) | async-done | bytes 3145744 | tf_op jit(solution)/shard_map/psum | solution.py:98
  (89 shorter events, 19.1 us)
Async XLA Ops:
  6.5 2.8 copy-start
  6.5 202.5 %all-gather.2.cloned.1.call-start = ((), (), s32[]{:S(2)}) async-start(), calls=%async_computation | async-start | bytes 1585152 | tf_op jit(solution)/shard_map/all_gather | solution.py:32
  7.3 2206.9 %all-reduce.3.cloned.1.call-start = ((), (), s32[]{:S(2)}) async-start(), calls=%async_computation.1 | async-start | bytes 6291456 | tf_op jit(solution)/shard_map/psum | solution.py:98
  15.0 1.0 copy-start.1
  15.0 1.1 copy-start.2
  15.0 1.4 copy-start.3
Sparse Core Ops, SparseCore 0:
  9.2 199.8 all-gather.1
  905.6 1308.4 all-reduce.2
where the time goes:
time: 2230 us; the launch traced here: 2220 us
  blocking collectives  1320 us (59%)
  waiting for transfers between devices  835 us (37%)
  matrix products  31.1 us (1%)
    psum x1, blocking collectives, body(): full_numerator, full_denominator = lax.psum((numerator, denominator), 'seq')  664 us
    pmax x1, blocking collectives, body(): row_max = lax.pmax(all_heads, 'seq')  659 us
    psum x1, waiting for transfers between devices, body(): full_numerator, full_denominator = lax.psum((numerator, denominator), 'seq')  643 us
    all_gather x1, waiting for transfers between devices, body(): everyone = lax.all_gather(queries, 'seq', axis=0, tiled=True)  191 us
  transfers between devices with their start and end apart: 2, of which 2 were waited for; matrix products, arithmetic and copies ran while one was open for 0% of the time, Pallas kernels for 0%

commit v1 on v0

v1 whole, which is shorter than its diff:
```python
import functools
import math

import jax
import jax.numpy as jnp
from jax import lax
from jax.experimental import pallas as pl
from jax.experimental.pallas import tpu as pltpu
from jax.sharding import PartitionSpec as P

F32 = jnp.float32
BF16 = jnp.bfloat16
HD = 128
COEF = HD ** -0.5 * math.log2(math.e)
BIG = 1e30
ROWS = 48
NT = (((1,), (1,)), ((), ()))


def lane_bcast(tile, k):
    return jnp.broadcast_to(tile[:, k : k + 1], (8, 128))


def merge_tiles(tiles):
    top = functools.reduce(jnp.maximum, tiles)
    scales = [jnp.exp2((t - top) * COEF) for t in tiles]
    total = sum(pltpu.roll(e, 64, 1) * t for e, t in zip(scales, tiles))
    lane = lax.broadcasted_iota(jnp.int32, (8, 128), 1)
    return jnp.where(lane < 64, top, total), scales


def scale_rows(scale, rows):
    n = rows.shape[0] // 8
    return jnp.concatenate([lane_bcast(scale, k) * rows[8 * k : 8 * k + 8] for k in range(n)], 0)


def kernel(
    q_hbm, root_hbm, doc_hbm, suf_hbm, new_hbm, len_hbm, rd_hbm, ol_hbm, dr_hbm,
    out_ref,
    qbuf, raw, f32s, keys, vals, suf, newb, newf, tail_s, len_s, rd_s, ol_s, dr_s,
    ns1, ss1, nr1, sr1, own2, ns2, ss2, nr2, sr2, own3, ns3, ss3, nr3, sr3,
    tail_num, tail_m, tail_l,
    lsem, kvs, kvr, zs, zr, bs, br_, as_, ar_, r1s, r1r, r2s, r2r, r3s, r3r,
):
    me = lax.axis_index("seq")
    core = lax.rem(me, 2)
    z = lax.rem(me // 2, 4)
    y = lax.rem(me // 8, 4)
    x = me // 32

    def dev(xx, yy, zz, cc):
        return {"seq": ((xx * 4 + yy) * 4 + zz) * 2 + cc}

    def zpeer(d):
        return dev(x, y, lax.rem(z + d, 4), core)

    def xpeer(d):
        return dev(lax.rem(x + d, 4), y, z, core)

    def ypeer(d):
        return dev(x, lax.rem(y + d, 4), z, core)

    apeer = (xpeer, ypeer)
    bpeer = (ypeer, xpeer)
    partner = dev(x, y, z, 1 - core)

    local = []

    def fetch(src, dst):
        c = pltpu.make_async_copy(src, dst, lsem.at[len(local)])
        c.start()
        local.append(c)
        return c

    c_q = fetch(q_hbm, qbuf.at[0, 0, 0, 0])
    c_root = fetch(root_hbm, raw.at[0, 0])
    c_doc = fetch(doc_hbm, raw.at[1, 0])
    c_ol = fetch(ol_hbm, ol_s)
    c_rd = fetch(rd_hbm, rd_s)
    c_dr = fetch(dr_hbm, dr_s)
    c_len = fetch(len_hbm, len_s)
    c_new = fetch(new_hbm, newb)
    c_suf = fetch(suf_hbm, suf)

    barrier = pltpu.get_barrier_semaphore()
    peers = [partner] + [f(d) for f in (zpeer, xpeer, ypeer) for d in (1, 2, 3)]
    for p in peers:
        pl.semaphore_signal(barrier, inc=1, device_id=p, device_id_type=pl.DeviceIdType.MESH)
    pl.semaphore_wait(barrier, len(peers))

    def send(src, dst, ss, rs, to):
        c = pltpu.make_async_remote_copy(
            src_ref=src, dst_ref=dst, send_sem=ss, recv_sem=rs,
            device_id=to, device_id_type=pl.DeviceIdType.MESH,
        )
        c.start()
        return c

    sent = []

    c_q.wait()
    for d in (1, 3, 2):
        r = 4 - d
        sent.append(send(qbuf.at[0, 0, 0, 0], qbuf.at[r // 2, 0, 0, r % 2], zs.at[d - 1], zr.at[r - 1], zpeer(d)))
    kv_root = send(root_hbm, raw.at[0, 1], kvs.at[0], kvr.at[0], partner)
    kv_doc = send(doc_hbm, raw.at[1, 1], kvs.at[1], kvr.at[1], partner)

    vals[:, :, HD:] = jnp.ones((2, 1024, HD), BF16)
    newf[...] = jnp.zeros_like(newf)

    def split_heads(src, who):
        for kv in range(2):
            f32s[src, who, kv] = raw[src, who, kv].astype(F32)
            base = src * 512 + who * 256
            for h in range(2):
                part = f32s[src, who, kv, pl.ds(h, 256, stride=2), :].astype(BF16)
                if kv == 0:
                    keys[h, base : base + 256] = part
                else:
                    vals[h, base : base + 256, :HD] = part

    c_root.wait()
    split_heads(0, 0)
    c_doc.wait()
    split_heads(1, 0)

    def wait_recv(dst, sem):
        pltpu.make_async_copy(dst, dst, sem).wait()

    for path, rels in ((0, (1,)), (1, (2, 3))):
        for r in rels:
            wait_recv(qbuf.at[r // 2, 0, 0, r % 2], zr.at[r - 1])
        for d in (1, 3, 2):
            r = 4 - d
            sent.append(send(qbuf.at[path, 0, 0], qbuf.at[path, 0, r], bs.at[path, d - 1], br_.at[path, r - 1], bpeer[path](d)))

    kv_root.wait_recv()
    split_heads(0, 1)
    kv_doc.wait_recv()
    split_heads(1, 1)

    for path in range(2):
        for r in (1, 3, 2):
            wait_recv(qbuf.at[path, 0, r], br_.at[path, r - 1])
        for d in (1, 3, 2):
            r = 4 - d
            sent.append(send(qbuf.at[path, 0], qbuf.at[path, r], as_.at[path, d - 1], ar_.at[path, r - 1], apeer[path](d)))

    for c in (c_ol, c_rd, c_dr, c_len, c_new, c_suf):
        c.wait()
    length = len_s[0]
    qown = qbuf[0, 0, 0, 0]
    row = lax.broadcasted_iota(jnp.int32, (ROWS, 1024), 0)
    col = lax.broadcasted_iota(jnp.int32, (ROWS, 1024), 1)
    same = (row // 8) % 2 == col % 2
    tops = []
    for c in range(4):
        s = lax.dot_general(qown, suf[0, 1024 * c : 1024 * c + 1024], NT, preferred_element_type=F32)
        s = jnp.where(same & (col // 2 < length - 512 * c), s, -BIG)
        tail_s[:, 1024 * c : 1024 * c + 1024] = s
        tops.append(jnp.max(s, 1, keepdims=True))
    for kv in range(2):
        for j in range(3):
            newf[kv, 2 * j : 2 * j + 2] = newb[kv, j].astype(F32)
    s_new = lax.dot_general(qown, newf[0].astype(BF16), NT, preferred_element_type=F32)
    r128, c128 = row[:, :128], col[:, :128]
    s_new = jnp.where(((r128 // 8) % 2 == c128 % 2) & (c128 // 2 <= r128 // 16) & (c128 < 6), s_new, -BIG)
    tops.append(jnp.max(s_new, 1, keepdims=True))
    top = functools.reduce(jnp.maximum, tops)
    p_new = jnp.exp2((s_new - top) * COEF).astype(BF16)
    num = lax.dot_general(p_new, newf[1].astype(BF16), (((1,), (0,)), ((), ())), preferred_element_type=F32)
    total = jnp.sum(p_new.astype(F32), 1, keepdims=True)
    for c in range(4):
        p = jnp.exp2((tail_s[:, 1024 * c : 1024 * c + 1024] - top) * COEF).astype(BF16)
        num += jnp.dot(p, suf[1, 1024 * c : 1024 * c + 1024], preferred_element_type=F32)
        total += jnp.sum(p.astype(F32), 1, keepdims=True)
    tail_num[...] = num
    tail_m[...] = jnp.broadcast_to(top, (ROWS, 128))
    tail_l[...] = jnp.broadcast_to(total, (ROWS, 128))

    lane = lax.broadcasted_iota(jnp.int32, (8, 128), 1)
    chip = me // 2

    def block(path, a_rel):
        q = qbuf[path, a_rel].reshape(8 * ROWS, HD).astype(F32).reshape(24, 2, 8, HD)
        bars = []
        for b_rel in range(4):
            for zz in range(2):
                aa, bb = (x, y) if path == 0 else (y, x)
                aa, bb = lax.rem(aa + a_rel, 4), lax.rem(bb + b_rel, 4)
                xx, yy = (aa, bb) if path == 0 else (bb, aa)
                slot = ((xx * 4 + yy) * 4 + lax.rem(z + 2 * path + zz, 4)) * 2 + core
                run = dr_s[rd_s[ol_s[slot]]]
                bars.append(jnp.full((24, 1), jnp.where(run == chip, 0.0, BIG), F32))
        bar = jnp.concatenate(bars, 0)
        nums, tile = [], jnp.zeros((8, 128), F32)
        for h in range(2):
            qh = q[:, h].reshape(24 * 8, HD).astype(BF16)
            s = lax.dot_general(qh, keys[h], NT, preferred_element_type=F32)
            s0, s1 = s[:, :512], s[:, 512:]
            m = jnp.maximum(jnp.max(s0, 1, keepdims=True), jnp.max(s1, 1, keepdims=True) - bar)
            p0 = jnp.exp2((s0 - m) * COEF).astype(BF16)
            p1 = jnp.exp2((s1 - (m + bar)) * COEF).astype(BF16)
            o = jnp.dot(p0, vals[h, :512], preferred_element_type=F32)
            o += jnp.dot(p1, vals[h, 512:], preferred_element_type=F32)
            nums.append(o[:, :HD].reshape(24, 1, 8, HD))
            for i in range(24):
                k = 2 * i + h
                tile = jnp.where(lane == k, m[8 * i : 8 * i + 8], tile)
                tile = jnp.where(lane == 64 + k, o[8 * i : 8 * i + 8, HD:], tile)
        ns1[path, a_rel] = jnp.concatenate(nums, 1).reshape(8 * ROWS, HD).astype(BF16)
        ss1[path, a_rel] = tile

    def rs1(path, d):
        r = lax.rem(4 - d, 4)
        to = apeer[path](d)
        return [
            pltpu.make_async_remote_copy(
                src_ref=ns1.at[path, d], dst_ref=nr1.at[path, r - 1], send_sem=r1s.at[path, d - 1, 0],
                recv_sem=r1r.at[path, r - 1, 0], device_id=to, device_id_type=pl.DeviceIdType.MESH),
            pltpu.make_async_remote_copy(
                src_ref=ss1.at[path, d], dst_ref=sr1.at[path, r - 1], send_sem=r1s.at[path, d - 1, 1],
                recv_sem=r1r.at[path, r - 1, 1], device_id=to, device_id_type=pl.DeviceIdType.MESH),
        ]

    def step(i, carry):
        a_rel = jnp.where(i == 2, 3, jnp.where(i == 3, 2, i))

        @pl.when(i > 0)
        def _():
            for path in range(2):
                wait_recv(qbuf.at[path, a_rel], ar_.at[path, a_rel - 1])

        for path in range(2):
            block(path, a_rel)

        @pl.when(i > 0)
        def _():
            for path in range(2):
                for c in rs1(path, a_rel):
                    c.start()

        return carry

    lax.fori_loop(0, 4, step, 0)

    for path in range(2):
        for r in (1, 3, 2):
            wait_recv(nr1.at[path, r - 1], r1r.at[path, r - 1, 0])
            wait_recv(sr1.at[path, r - 1], r1r.at[path, r - 1, 1])
        tile, scales = merge_tiles([ss1[path, 0]] + [sr1[path, r] for r in range(3)])
        acc = scale_rows(scales[0], ns1[path, 0].astype(F32))
        for r in range(3):
            acc += scale_rows(scales[r + 1], nr1[path, r].astype(F32))
        own2[path] = acc[:96]
        for d in range(3):
            ns2[path, d] = acc[96 * (d + 1) : 96 * (d + 2)].astype(BF16)
        ss2[path] = tile
        for d in (1, 3, 2):
            r = 4 - d
            sent.append(send(ns2.at[path, d - 1], nr2.at[path, r - 1], r2s.at[path, d - 1, 0], r2r.at[path, r - 1, 0], bpeer[path](d)))
            sent.append(send(ss2.at[path], sr2.at[path, r - 1], r2s.at[path, d - 1, 1], r2r.at[path, r - 1, 1], bpeer[path](d)))

    for path in (1, 0):
        for r in (1, 3, 2):
            wait_recv(nr2.at[path, r - 1], r2r.at[path, r - 1, 0])
            wait_recv(sr2.at[path, r - 1], r2r.at[path, r - 1, 1])
        tiles = [ss2[path]] + [pltpu.roll(sr2[path, r - 1], 128 - 12 * (4 - r), 1) for r in (1, 2, 3)]
        tile, scales = merge_tiles(tiles)
        acc = scale_rows(scales[0][:, :], own2[path])
        for r in range(3):
            acc += scale_rows(scales[r + 1], nr2[path, r].astype(F32))
        for zz in range(2):
            d = 2 * path + zz
            if d == 0:
                own3[...] = acc[:ROWS]
            else:
                ns3[d - 1] = acc[ROWS * zz : ROWS * zz + ROWS].astype(BF16)
        ss3[path] = tile
        for zz in (1, 0):
            d = 2 * path + zz
            if d:
                r = 4 - d
                sent.append(send(ns3.at[d - 1], nr3.at[r - 1], r3s.at[d - 1, 0], r3r.at[r - 1, 0], zpeer(d)))
                sent.append(send(ss3.at[path], sr3.at[r - 1], r3s.at[d - 1, 1], r3r.at[r - 1, 1], zpeer(d)))

    for r in (1, 2, 3):
        wait_recv(nr3.at[r - 1], r3r.at[r - 1, 0])
        wait_recv(sr3.at[r - 1], r3r.at[r - 1, 1])
    tiles = [ss3[0]]
    for r in (1, 2, 3):
        t = sr3[r - 1]
        tiles.append(pltpu.roll(t, 128 - 6, 1) if (4 - r) % 2 else t)
    parts = [(own3[...], tiles[0])] + [(nr3[r].astype(F32), tiles[r + 1]) for r in range(3)]
    for k in range(6):
        at = slice(8 * k, 8 * k + 8)
        tops = [lane_bcast(t, k) for _, t in parts] + [tail_m[at]]
        sums = [lane_bcast(t, 64 + k) for _, t in parts] + [tail_l[at]]
        vals_k = [n[at] for n, _ in parts] + [tail_num[at]]
        top = functools.reduce(jnp.maximum, tops)
        es = [jnp.exp2((t - top) * COEF) for t in tops]
        den = sum(e * s for e, s in zip(es, sums))
        num = sum(e * v for e, v in zip(es, vals_k))
        tail_num[at] = num / den
    out_ref[...] = tail_num[...].astype(BF16)

    for c in sent:
        c.wait_send()
    kv_root.wait_send()
    kv_doc.wait_send()
    for path in range(2):
        for d in (1, 2, 3):
            for c in rs1(path, d):
                c.wait_send()


def body(queries, root_kv, doc_kv, suffix_kv, new_kv, suffix_len, request_doc, owner_list, doc_run):
    vm, dma = pltpu.VMEM, pltpu.SemaphoreType.DMA
    any_spec = pl.BlockSpec(memory_space=pl.ANY)
    out = pl.pallas_call(
        kernel,
        out_shape=jax.ShapeDtypeStruct((ROWS, HD), BF16),
        in_specs=[any_spec] * 9,
        out_specs=pl.BlockSpec(memory_space=pltpu.VMEM),
        scratch_shapes=[
            vm((2, 4, 4, 2, ROWS, HD), BF16),
            vm((2, 2, 2, 512, HD), BF16),
            vm((2, 2, 2, 512, HD), F32),
            vm((2, 1024, HD), BF16),
            vm((2, 1024, 2 * HD), BF16),
            vm((2, 4096, HD), BF16),
            vm((2, 3, 2, HD), BF16),
            vm((2, 128, HD), F32),
            vm((ROWS, 4096), F32),
            pltpu.SMEM((1,), jnp.int32),
            pltpu.SMEM((128,), jnp.int32),
            pltpu.SMEM((128,), jnp.int32),
            pltpu.SMEM((64,), jnp.int32),
            vm((2, 4, 8 * ROWS, HD), BF16),
            vm((2, 4, 8, 128), F32),
            vm((2, 3, 8 * ROWS, HD), BF16),
            vm((2, 3, 8, 128), F32),
            vm((2, 96, HD), F32),
            vm((2, 3, 96, HD), BF16),
            vm((2, 8, 128), F32),
            vm((2, 3, 96, HD), BF16),
            vm((2, 3, 8, 128), F32),
            vm((ROWS, HD), F32),
            vm((3, ROWS, HD), BF16),
            vm((2, 8, 128), F32),
            vm((3, ROWS, HD), BF16),
            vm((3, 8, 128), F32),
            vm((ROWS, HD), F32),
            vm((ROWS, HD), F32),
            vm((ROWS, HD), F32),
            dma((9,)),
            dma((2,)), dma((2,)),
            dma((3,)), dma((3,)),
            dma((2, 3)), dma((2, 3)),
            dma((2, 3)), dma((2, 3)),
            dma((2, 3, 2)), dma((2, 3, 2)),
            dma((2, 3, 2)), dma((2, 3, 2)),
            dma((3, 2)), dma((3, 2)),
        ],
        compiler_params=pltpu.CompilerParams(
            collective_id=0, has_side_effects=True, vmem_limit_bytes=40 * 1024 * 1024
        ),
    )(
        queries.reshape(ROWS, HD),
        root_kv.reshape(2, 512, HD),
        doc_kv.reshape(2, 512, HD),
        suffix_kv.reshape(2, 4096, HD),
        new_kv.reshape(2, 3, 2, HD),
        suffix_len,
        request_doc.reshape(128),
        owner_list,
        doc_run,
    )
    return out.reshape(1, 3, 2048)


def solution(mesh):
    in_specs = (
        P("seq", None, "kvh", None, None),
        P(None, "seq", "kvh", None),
        P(None, "seq", "kvh", None),
        P(None, "seq", None, "kvh", None),
        P(None, "seq", None, "kvh", None),
        P("seq"),
        P(),
        P(),
        P(),
    )
    out_specs = P("seq", None, "kvh")
    return jax.shard_map(body, mesh=mesh, in_specs=in_specs, out_specs=out_specs, check_vma=False)
```

time: 2230 us -> 47.1 us (0.02)
  the two profiles are of different devices: /device:TPU:1 before, /device:TPU:8 now
where the time goes in v1:
time: 47.1 us; the launch traced here: 46.8 us
  Pallas kernels  38.7 us (82%)
  local copies, waits for them, and re-layouts  7.45 us (16%)
  between operations  0.68 us (1%)
    pallas_call x1, Pallas kernels, body(): pl.pallas_call(kernel, out_shape=jax.ShapeDtypeStruct((ROWS, HD), BF16),...  38.7 us
    unnamed x16, local copies, waits for them, and re-layouts  6.84 us

profile of v1, /device:TPU:8, one launch (start us, length us, event | category | flops | bytes accessed | tf_op | source)
XLA Modules:
  0.0 46.8 jit_solution(11590825726061274472)
XLA Ops:
  0.7 0.0 copy-start
  0.7 1.6 %copy-done = bf16[2,1,2048,2,128]{4,3,2,1,0:T(2,128)(2,1)S(1)} copy-done((bf16[2,1,2048,2,128]{4,3,2,1,0:T(2,128)(2,1)S(1)}, bf16[2,1,2048,2,128]{4,3,2,1,0:T(2,128)(2,1)}, u32[]{:S(2)}) %copy-start) | copy-done | bytes 2097176
  2.2 0.0 copy-start.1
  2.2 0.9 %copy-done.1 = bf16[2,256,2,128]{3,2,1,0:T(2,128)(2,1)S(1)} copy-done((bf16[2,256,2,128]{3,2,1,0:T(2,128)(2,1)S(1)}, bf16[2,256,2,128]{3,2,1,0:T(2,128)(2,1)}, u32[]{:S(2)}) %copy-start.1) | copy-done | bytes 262168
  3.2 0.0 copy-start.2
  3.2 0.9 %copy-done.2 = bf16[2,256,2,128]{3,2,1,0:T(2,128)(2,1)S(1)} copy-done((bf16[2,256,2,128]{3,2,1,0:T(2,128)(2,1)S(1)}, bf16[2,256,2,128]{3,2,1,0:T(2,128)(2,1)}, u32[]{:S(2)}) %copy-start.2) | copy-done | bytes 262168
  4.1 0.0 copy-start.3
  4.1 0.7 %copy-done.3 = bf16[1,3,2,8,128]{4,3,2,1,0:T(8,128)(2,1)S(1)} copy-done((bf16[1,3,2,8,128]{4,3,2,1,0:T(8,128)(2,1)S(1)}, bf16[1,3,2,8,128]{4,3,2,1,0:T(8,128)(2,1)}, u32[]{:S(2)}) %copy-start.3) | copy-done | bytes 12312
  4.9 0.0 copy-start.4
  4.9 0.7 %copy-done.4 = bf16[2,1,3,2,128]{4,3,2,1,0:T(2,128)(2,1)S(1)} copy-done((bf16[2,1,3,2,128]{4,3,2,1,0:T(2,128)(2,1)S(1)}, bf16[2,1,3,2,128]{4,3,2,1,0:T(2,128)(2,1)}, u32[]{:S(2)}) %copy-start.4) | copy-done | bytes 3096
  5.5 0.0 copy-start.5
  5.5 0.7 %copy-done.5 = s32[128,1]{0,1:T(1,128)S(1)} copy-done((s32[128,1]{0,1:T(1,128)S(1)}, s32[128,1]{0,1:T(1,128)}, u32[]{:S(2)}) %copy-start.5) | copy-done | bytes 536
  6.2 0.0 copy-start.6
  6.2 0.7 %copy-done.6 = s32[128]{0:T(128)S(1)} copy-done((s32[128]{0:T(128)S(1)}, s32[128]{0:T(128)}, u32[]{:S(2)}) %copy-start.6) | copy-done | bytes 536
  6.8 0.0 copy-start.7
  6.9 0.7 %copy-done.7 = s32[64]{0:T(128)S(1)} copy-done((s32[64]{0:T(128)S(1)}, s32[64]{0:T(128)}, u32[]{:S(2)}) %copy-start.7) | copy-done | bytes 280
  7.5 38.7 %shard_map.91 = bf16[48,128]{1,0:T(8,128)(2,1)S(1)} custom-call(bf16[48,128]{1,0:T(8,128)(2,1)S(1)} %bitcast.9, bf16[2,512,128]{2,1,0:T(8,128)(2,1)S(1)} %bitcast.7, bf16[2,512,128]{2,1,0:T(8,128)(2,1)S(1)} %bitcast.8, bf16[2,4096,128]{2,1,0:T(8,128)(2,1)S(1)} %bitcast.6, bf16[2,3,2,128]{3,2,1,0:T(2,128)(2,1)S(1)} %bitcast.10, s32[1]{0:T(128)S(6)} %copy.10.len_hbm, ...), custom_call_target="tpu_custom_call" | custom-call | tf_op jit(solution)/shard_map/pallas_call | solution.py:320
  46.2 0.6 %reshape.27 = bf16[1,3,2048]{2,1,0:T(4,128)(2,1)} reshape(bf16[48,128]{1,0:T(8,128)(2,1)S(1)} %shard_map.91) | data formatting | bytes 24576 | tf_op jit(solution)/shard_map/reshape | solution.py:379
Async XLA Ops:
  0.7 1.6 %copy-start = (bf16[2,1,2048,2,128]{4,3,2,1,0:T(2,128)(2,1)S(1)}, bf16[2,1,2048,2,128]{4,3,2,1,0:T(2,128)(2,1)}, u32[]{:S(2)}) copy-start(bf16[2,1,2048,2,128]{4,3,2,1,0:T(2,128)(2,1)} %param.12) | copy-start | bytes 6291460
  2.2 0.9 %copy-start.1 = (bf16[2,256,2,128]{3,2,1,0:T(2,128)(2,1)S(1)}, bf16[2,256,2,128]{3,2,1,0:T(2,128)(2,1)}, u32[]{:S(2)}) copy-start(bf16[2,256,2,128]{3,2,1,0:T(2,128)(2,1)} %param.10) | copy-start | bytes 786436
  3.2 0.9 %copy-start.2 = (bf16[2,256,2,128]{3,2,1,0:T(2,128)(2,1)S(1)}, bf16[2,256,2,128]{3,2,1,0:T(2,128)(2,1)}, u32[]{:S(2)}) copy-start(bf16[2,256,2,128]{3,2,1,0:T(2,128)(2,1)} %param.11) | copy-start | bytes 786436
  4.1 0.7 %copy-start.3 = (bf16[1,3,2,8,128]{4,3,2,1,0:T(8,128)(2,1)S(1)}, bf16[1,3,2,8,128]{4,3,2,1,0:T(8,128)(2,1)}, u32[]{:S(2)}) copy-start(bf16[1,3,2,8,128]{4,3,2,1,0:T(8,128)(2,1)} %param.9) | copy-start | bytes 36868
  4.9 0.7 %copy-start.4 = (bf16[2,1,3,2,128]{4,3,2,1,0:T(2,128)(2,1)S(1)}, bf16[2,1,3,2,128]{4,3,2,1,0:T(2,128)(2,1)}, u32[]{:S(2)}) copy-start(bf16[2,1,3,2,128]{4,3,2,1,0:T(2,128)(2,1)} %param.13) | copy-start | bytes 9220
  5.5 0.7 %copy-start.5 = (s32[128,1]{0,1:T(1,128)S(1)}, s32[128,1]{0,1:T(1,128)}, u32[]{:S(2)}) copy-start(s32[128,1]{0,1:T(1,128)} %param.15) | copy-start | bytes 1540
  6.2 0.7 %copy-start.6 = (s32[128]{0:T(128)S(1)}, s32[128]{0:T(128)}, u32[]{:S(2)}) copy-start(s32[128]{0:T(128)} %ol_hbm.1) | copy-start | bytes 1540
  6.8 0.7 %copy-start.7 = (s32[64]{0:T(128)S(1)}, s32[64]{0:T(128)}, u32[]{:S(2)}) copy-start(s32[64]{0:T(128)} %dr_hbm.1) | copy-start | bytes 772

commit v2 on v1

--- a/solution.py
+++ b/solution.py
@@ -29,6 +29,16 @@
     return jnp.where(lane < 64, top, total), scales
 
 
+def pack_tile(tile):
+    high = tile.astype(BF16).astype(F32)
+    return jnp.concatenate([high, tile - high], 0).astype(BF16)
+
+
+def unpack_tile(rows):
+    rows = rows.astype(F32)
+    return rows[:8] + rows[8:]
+
+
 def scale_rows(scale, rows):
     n = rows.shape[0] // 8
     return jnp.concatenate([lane_bcast(scale, k) * rows[8 * k : 8 * k + 8] for k in range(n)], 0)
@@ -38,7 +48,7 @@
     q_hbm, root_hbm, doc_hbm, suf_hbm, new_hbm, len_hbm, rd_hbm, ol_hbm, dr_hbm,
     out_ref,
     qbuf, raw, f32s, keys, vals, suf, newb, newf, tail_s, len_s, rd_s, ol_s, dr_s,
-    ns1, ss1, nr1, sr1, own2, ns2, ss2, nr2, sr2, own3, ns3, ss3, nr3, sr3,
+    ns1, nr1, own2, ns2, ss2, nr2, own3, ns3, ss3, nr3,
     tail_num, tail_m, tail_l,
     lsem, kvs, kvr, zs, zr, bs, br_, as_, ar_, r1s, r1r, r2s, r2r, r3s, r3r,
 ):
@@ -98,10 +108,30 @@
 
     sent = []
 
+    def to_b(path, zz):
+        for d in (2, 1, 3):
+            r = 4 - d
+            sent.append(send(qbuf.at[path, 0, 0, zz], qbuf.at[path, 0, r, zz], bs.at[path, d - 1, zz], br_.at[path, r - 1, zz], bpeer[path](d)))
+
+    def to_a(path, zz):
+        for d in (2, 1, 3):
+            r = 4 - d
+            sent.append(send(qbuf.at[path, 0, 0, zz], qbuf.at[path, r, 0, zz], as_.at[path, d - 1, zz], ar_.at[path, r - 1, zz], apeer[path](d)))
+
+    def on_to_a(path, b_rel):
+        for d in (2, 1, 3):
+            r = 4 - d
+            sent.append(send(qbuf.at[path, 0, b_rel], qbuf.at[path, r, b_rel], as_.at[path, d - 1, b_rel + 1], ar_.at[path, r - 1, b_rel + 1], apeer[path](d)))
+
+    def wait_recv(dst, sem):
+        pltpu.make_async_copy(dst, dst, sem).wait()
+
     c_q.wait()
-    for d in (1, 3, 2):
+    for d in (2, 1, 3):
         r = 4 - d
         sent.append(send(qbuf.at[0, 0, 0, 0], qbuf.at[r // 2, 0, 0, r % 2], zs.at[d - 1], zr.at[r - 1], zpeer(d)))
+    to_b(0, 0)
+    to_a(0, 0)
     kv_root = send(root_hbm, raw.at[0, 1], kvs.at[0], kvr.at[0], partner)
     kv_doc = send(doc_hbm, raw.at[1, 1], kvs.at[1], kvr.at[1], partner)
 
@@ -124,15 +154,11 @@
     c_doc.wait()
     split_heads(1, 0)
 
-    def wait_recv(dst, sem):
-        pltpu.make_async_copy(dst, dst, sem).wait()
-
-    for path, rels in ((0, (1,)), (1, (2, 3))):
-        for r in rels:
-            wait_recv(qbuf.at[r // 2, 0, 0, r % 2], zr.at[r - 1])
-        for d in (1, 3, 2):
-            r = 4 - d
-            sent.append(send(qbuf.at[path, 0, 0], qbuf.at[path, 0, r], bs.at[path, d - 1], br_.at[path, r - 1], bpeer[path](d)))
+    for r in (1, 3, 2):
+        path, zz = r // 2, r % 2
+        wait_recv(qbuf.at[path, 0, 0, zz], zr.at[r - 1])
+        to_b(path, zz)
+        to_a(path, zz)
 
     kv_root.wait_recv()
     split_heads(0, 1)
@@ -141,10 +167,9 @@
 
     for path in range(2):
         for r in (1, 3, 2):
-            wait_recv(qbuf.at[path, 0, r], br_.at[path, r - 1])
-        for d in (1, 3, 2):
-            r = 4 - d
-            sent.append(send(qbuf.at[path, 0], qbuf.at[path, r], as_.at[path, d - 1], ar_.at[path, r - 1], apeer[path](d)))
+            for zz in range(2):
+                wait_recv(qbuf.at[path, 0, r, zz], br_.at[path, r - 1, zz])
+            on_to_a(path, r)
 
     for c in (c_ol, c_rd, c_dr, c_len, c_new, c_suf):
         c.wait()
@@ -186,9 +211,8 @@
         bars = []
         for b_rel in range(4):
             for zz in range(2):
-                aa, bb = (x, y) if path == 0 else (y, x)
-                aa, bb = lax.rem(aa + a_rel, 4), lax.rem(bb + b_rel, 4)
-                xx, yy = (aa, bb) if path == 0 else (bb, aa)
+                xx = lax.rem(x + jnp.where(path == 0, a_rel, b_rel), 4)
+                yy = lax.rem(y + jnp.where(path == 0, b_rel, a_rel), 4)
                 slot = ((xx * 4 + yy) * 4 + lax.rem(z + 2 * path + zz, 4)) * 2 + core
                 run = dr_s[rd_s[ol_s[slot]]]
                 bars.append(jnp.full((24, 1), jnp.where(run == chip, 0.0, BIG), F32))
@@ -199,6 +223,7 @@
             s = lax.dot_general(qh, keys[h], NT, preferred_element_type=F32)
             s0, s1 = s[:, :512], s[:, 512:]
             m = jnp.maximum(jnp.max(s0, 1, keepdims=True), jnp.max(s1, 1, keepdims=True) - bar)
+            m = m.astype(BF16).astype(F32)
             p0 = jnp.exp2((s0 - m) * COEF).astype(BF16)
             p1 = jnp.exp2((s1 - (m + bar)) * COEF).astype(BF16)
             o = jnp.dot(p0, vals[h, :512], preferred_element_type=F32)
@@ -208,101 +233,90 @@
                 k = 2 * i + h
                 tile = jnp.where(lane == k, m[8 * i : 8 * i + 8], tile)
                 tile = jnp.where(lane == 64 + k, o[8 * i : 8 * i + 8, HD:], tile)
-        ns1[path, a_rel] = jnp.concatenate(nums, 1).reshape(8 * ROWS, HD).astype(BF16)
-        ss1[path, a_rel] = tile
+        ns1[path, a_rel, : 8 * ROWS] = jnp.concatenate(nums, 1).reshape(8 * ROWS, HD).astype(BF16)
+        ns1[path, a_rel, 8 * ROWS :] = pack_tile(tile)
 
     def rs1(path, d):
         r = lax.rem(4 - d, 4)
-        to = apeer[path](d)
-        return [
-            pltpu.make_async_remote_copy(
-                src_ref=ns1.at[path, d], dst_ref=nr1.at[path, r - 1], send_sem=r1s.at[path, d - 1, 0],
-                recv_sem=r1r.at[path, r - 1, 0], device_id=to, device_id_type=pl.DeviceIdType.MESH),
-            pltpu.make_async_remote_copy(
-                src_ref=ss1.at[path, d], dst_ref=sr1.at[path, r - 1], send_sem=r1s.at[path, d - 1, 1],
-                recv_sem=r1r.at[path, r - 1, 1], device_id=to, device_id_type=pl.DeviceIdType.MESH),
-        ]
+        xx = lax.rem(x + jnp.where(path == 0, d, 0), 4)
+        yy = lax.rem(y + jnp.where(path == 0, 0, d), 4)
+        return pltpu.make_async_remote_copy(
+            src_ref=ns1.at[path, d], dst_ref=nr1.at[path, r - 1], send_sem=r1s.at[path, d - 1],
+            recv_sem=r1r.at[path, r - 1], device_id=dev(xx, yy, z, core), device_id_type=pl.DeviceIdType.MESH)
 
     def step(i, carry):
-        a_rel = jnp.where(i == 2, 3, jnp.where(i == 3, 2, i))
-
-        @pl.when(i > 0)
+        path = jnp.where(i < 2, i, (i - 2) // 3)
+        k = lax.rem(i - 2, 3)
+        a_rel = jnp.where(i < 2, 0, jnp.where(k == 0, 1, 4 - k))
+
+        @pl.when(i >= 2)
         def _():
-            for path in range(2):
-                wait_recv(qbuf.at[path, a_rel], ar_.at[path, a_rel - 1])
-
-        for path in range(2):
-            block(path, a_rel)
-
-        @pl.when(i > 0)
+            for zz in range(2):
+                wait_recv(qbuf.at[path, a_rel, 0, zz], ar_.at[path, a_rel - 1, zz])
+            for b_rel in range(1, 4):
+                wait_recv(qbuf.at[path, a_rel, b_rel], ar_.at[path, a_rel - 1, b_rel + 1])
+
+        block(path, a_rel)
+
+        @pl.when(i >= 2)
         def _():
-            for path in range(2):
-                for c in rs1(path, a_rel):
-                    c.start()
+            rs1(path, a_rel).start()
 
         return carry
 
-    lax.fori_loop(0, 4, step, 0)
+    lax.fori_loop(0, 8, step, 0)
 
     for path in range(2):
         for r in (1, 3, 2):
-            wait_recv(nr1.at[path, r - 1], r1r.at[path, r - 1, 0])
-            wait_recv(sr1.at[path, r - 1], r1r.at[path, r - 1, 1])
-        tile, scales = merge_tiles([ss1[path, 0]] + [sr1[path, r] for r in range(3)])
-        acc = scale_rows(scales[0], ns1[path, 0].astype(F32))
+            wait_recv(nr1.at[path, r - 1], r1r.at[path, r - 1])
+        parts = [ns1.at[path, 0]] + [nr1.at[path, r] for r in range(3)]
+        tile, scales = merge_tiles([unpack_tile(p[8 * ROWS :]) for p in parts])
+        acc = sum(scale_rows(e, p[: 8 * ROWS].astype(F32)) for e, p in zip(scales, parts))
+        own2[path] = acc[:96]
+        ss2[path] = tile
+        for d in (2, 1, 3):
+            r = 4 - d
+            ns2[path, d - 1, :96] = acc[96 * d : 96 * (d + 1)].astype(BF16)
+            ns2[path, d - 1, 96:] = pack_tile(tile)
+            sent.append(send(ns2.at[path, d - 1], nr2.at[path, r - 1], r2s.at[path, d - 1], r2r.at[path, r - 1], bpeer[path](d)))
+
+    for path in range(2):
+        for r in (1, 3, 2):
+            wait_recv(nr2.at[path, r - 1], r2r.at[path, r - 1])
+        tiles = [ss2[path]] + [pltpu.roll(unpack_tile(nr2[path, r - 1, 96:]), 128 - 12 * (4 - r), 1) for r in (1, 2, 3)]
+        tile, scales = merge_tiles(tiles)
+        acc = scale_rows(scales[0], own2[path])
         for r in range(3):
-            acc += scale_rows(scales[r + 1], nr1[path, r].astype(F32))
-        own2[path] = acc[:96]
-        for d in range(3):
-            ns2[path, d] = acc[96 * (d + 1) : 96 * (d + 2)].astype(BF16)
-        ss2[path] = tile
-        for d in (1, 3, 2):
-            r = 4 - d
-            sent.append(send(ns2.at[path, d - 1], nr2.at[path, r - 1], r2s.at[path, d - 1, 0], r2r.at[path, r - 1, 0], bpeer[path](d)))
-            sent.append(send(ss2.at[path], sr2.at[path, r - 1], r2s.at[path, d - 1, 1], r2r.at[path, r - 1, 1], bpeer[path](d)))
-
-    for path in (1, 0):
-        for r in (1, 3, 2):
-            wait_recv(nr2.at[path, r - 1], r2r.at[path, r - 1, 0])
-            wait_recv(sr2.at[path, r - 1], r2r.at[path, r - 1, 1])
-        tiles = [ss2[path]] + [pltpu.roll(sr2[path, r - 1], 128 - 12 * (4 - r), 1) for r in (1, 2, 3)]
-        tile, scales = merge_tiles(tiles)
-        acc = scale_rows(scales[0][:, :], own2[path])
-        for r in range(3):
-            acc += scale_rows(scales[r + 1], nr2[path, r].astype(F32))
+            acc += scale_rows(scales[r + 1], nr2[path, r, :96].astype(F32))
+        if path == 0:
+            own3[...] = acc[:ROWS]
+            ss3[...] = tile
         for zz in range(2):
-            d = 2 * path + zz
-            if d == 0:
-                own3[...] = acc[:ROWS]
-            else:
-                ns3[d - 1] = acc[ROWS * zz : ROWS * zz + ROWS].astype(BF16)
-        ss3[path] = tile
-        for zz in (1, 0):
             d = 2 * path + zz
             if d:
                 r = 4 - d
-                sent.append(send(ns3.at[d - 1], nr3.at[r - 1], r3s.at[d - 1, 0], r3r.at[r - 1, 0], zpeer(d)))
-                sent.append(send(ss3.at[path], sr3.at[r - 1], r3s.at[d - 1, 1], r3r.at[r - 1, 1], zpeer(d)))
-
+                ns3[d - 1, :ROWS] = acc[ROWS * zz : ROWS * zz + ROWS].astype(BF16)
+                ns3[d - 1, ROWS:] = pack_tile(tile)
+                sent.append(send(ns3.at[d - 1], nr3.at[r - 1], r3s.at[d - 1], r3r.at[r - 1], zpeer(d)))
+
+    for r in (3, 1, 2):
+        wait_recv(nr3.at[r - 1], r3r.at[r - 1])
+    parts = [(own3[...], ss3[...])]
     for r in (1, 2, 3):
-        wait_recv(nr3.at[r - 1], r3r.at[r - 1, 0])
-        wait_recv(sr3.at[r - 1], r3r.at[r - 1, 1])
-    tiles = [ss3[0]]
-    for r in (1, 2, 3):
-        t = sr3[r - 1]
-        tiles.append(pltpu.roll(t, 128 - 6, 1) if (4 - r) % 2 else t)
-    parts = [(own3[...], tiles[0])] + [(nr3[r].astype(F32), tiles[r + 1]) for r in range(3)]
+        t = unpack_tile(nr3[r - 1, ROWS:])
+        parts.append((nr3[r - 1, :ROWS].astype(F32), pltpu.roll(t, 128 - 6, 1) if r % 2 else t))
     for k in range(6):
         at = slice(8 * k, 8 * k + 8)
         tops = [lane_bcast(t, k) for _, t in parts] + [tail_m[at]]
         sums = [lane_bcast(t, 64 + k) for _, t in parts] + [tail_l[at]]
-        vals_k = [n[at] for n, _ in parts] + [tail_num[at]]
+        nums = [n[at] for n, _ in parts] + [tail_num[at]]
         top = functools.reduce(jnp.maximum, tops)
         es = [jnp.exp2((t - top) * COEF) for t in tops]
         den = sum(e * s for e, s in zip(es, sums))
-        num = sum(e * v for e, v in zip(es, vals_k))
-        tail_num[at] = num / den
-    out_ref[...] = tail_num[...].astype(BF16)
+        res = sum(e * v for e, v in zip(es, nums)) / den
+        for g in range(8):
+            col = (8 * (k % 2) + g) * HD
+            out_ref[0, k // 2 : k // 2 + 1, col : col + HD] = res[g : g + 1].astype(BF16)
 
     for c in sent:
         c.wait_send()
@@ -310,16 +324,15 @@
     kv_doc.wait_send()
     for path in range(2):
         for d in (1, 2, 3):
-            for c in rs1(path, d):
-                c.wait_send()
+            rs1(path, d).wait_send()
 
 
 def body(queries, root_kv, doc_kv, suffix_kv, new_kv, suffix_len, request_doc, owner_list, doc_run):
     vm, dma = pltpu.VMEM, pltpu.SemaphoreType.DMA
-    any_spec = pl.BlockSpec(memory_space=pl.ANY)
+    any_spec = pl.BlockSpec(memory_space=pltpu.HBM)
     out = pl.pallas_call(
         kernel,
-        out_shape=jax.ShapeDtypeStruct((ROWS, HD), BF16),
+        out_shape=jax.ShapeDtypeStruct((1, 3, 2048), BF16),
         in_specs=[any_spec] * 9,
         out_specs=pl.BlockSpec(memory_space=pltpu.VMEM),
         scratch_shapes=[
@@ -336,34 +349,30 @@
             pltpu.SMEM((128,), jnp.int32),
             pltpu.SMEM((128,), jnp.int32),
             pltpu.SMEM((64,), jnp.int32),
-            vm((2, 4, 8 * ROWS, HD), BF16),
-            vm((2, 4, 8, 128), F32),
-            vm((2, 3, 8 * ROWS, HD), BF16),
-            vm((2, 3, 8, 128), F32),
+            vm((2, 4, 8 * ROWS + 16, HD), BF16),
+            vm((2, 3, 8 * ROWS + 16, HD), BF16),
             vm((2, 96, HD), F32),
-            vm((2, 3, 96, HD), BF16),
+            vm((2, 3, 112, HD), BF16),
             vm((2, 8, 128), F32),
-            vm((2, 3, 96, HD), BF16),
-            vm((2, 3, 8, 128), F32),
+            vm((2, 3, 112, HD), BF16),
             vm((ROWS, HD), F32),
-            vm((3, ROWS, HD), BF16),
-            vm((2, 8, 128), F32),
-            vm((3, ROWS, HD), BF16),
-            vm((3, 8, 128), F32),
+            vm((3, 64, HD), BF16),
+            vm((8, 128), F32),
+            vm((3, 64, HD), BF16),
             vm((ROWS, HD), F32),
             vm((ROWS, HD), F32),
             vm((ROWS, HD), F32),
             dma((9,)),
             dma((2,)), dma((2,)),
             dma((3,)), dma((3,)),
+            dma((2, 3, 2)), dma((2, 3, 2)),
+            dma((2, 3, 5)), dma((2, 3, 5)),
             dma((2, 3)), dma((2, 3)),
             dma((2, 3)), dma((2, 3)),
-            dma((2, 3, 2)), dma((2, 3, 2)),
-            dma((2, 3, 2)), dma((2, 3, 2)),
-            dma((3, 2)), dma((3, 2)),
+            dma((3,)), dma((3,)),
         ],
         compiler_params=pltpu.CompilerParams(
-            collective_id=0, has_side_effects=True, vmem_limit_bytes=40 * 1024 * 1024
+            collective_id=0, has_side_effects=True, vmem_limit_bytes=60 * 1024 * 1024
         ),
     )(
         queries.reshape(ROWS, HD),
@@ -376,7 +385,7 @@
         owner_list,
         doc_run,
     )
-    return out.reshape(1, 3, 2048)
+    return out
 
 
 def solution(mesh):

time: 47.1 us -> 40.9 us (0.87)
  the two profiles are of different devices: /device:TPU:8 before, /device:TPU:32 now
where the time goes in v2:
time: 40.9 us; the launch traced here: 40.7 us
  Pallas kernels  38.7 us (95%)
  local copies, waits for them, and re-layouts  1.33 us (3%)
  between operations  0.66 us (2%)
    pallas_call x1, Pallas kernels, body(): pl.pallas_call(kernel, out_shape=jax.ShapeDtypeStruct((1, 3, 2048), BF16)...  38.7 us
    unnamed x1, local copies, waits for them, and re-layouts  1.33 us

profile of v2, /device:TPU:32, one launch (start us, length us, event | category | flops | bytes accessed | tf_op | source)
XLA Modules:
  0.0 40.7 jit_solution(17328320614600368764)
XLA Ops:
  0.7 38.7 %shard_map.91 = bf16[1,3,2048]{2,1,0:T(4,128)(2,1)} custom-call(bf16[48,128]{1,0:T(8,128)(2,1)} %bitcast.9, bf16[2,512,128]{2,1,0:T(8,128)(2,1)} %bitcast.7, bf16[2,512,128]{2,1,0:T(8,128)(2,1)} %bitcast.8, bf16[2,4096,128]{2,1,0:T(8,128)(2,1)} %bitcast.6, bf16[2,3,2,128]{3,2,1,0:T(2,128)(2,1)} %bitcast.10, s32[1]{0:T(128)S(6)} %copy.11.len_hbm, ...), custom_call_target="tpu_custom_call" | custom-call | tf_op jit(solution)/shard_map/pallas_call | solution.py:333
  39.4 1.3 %copy.12 = bf16[1,3,2048]{2,1,0:T(4,128)(2,1)} copy(bf16[1,3,2048]{2,1,0:T(4,128)(2,1)} %shard_map.91) | data formatting | bytes 24576

commit v3 on v2

v3 whole, which is shorter than its diff:
```python
import functools
import math

import jax
import jax.numpy as jnp
from jax import lax
from jax.experimental import pallas as pl
from jax.experimental.pallas import tpu as pltpu
from jax.sharding import PartitionSpec as P

F32 = jnp.float32
BF16 = jnp.bfloat16
HD = 128
COEF = HD ** -0.5 * math.log2(math.e)
BIG = 1e30
ROWS = 48
NT = (((1,), (1,)), ((), ()))


def lane_bcast(tile, k):
    return jnp.broadcast_to(tile[:, k : k + 1], (8, 128))


def merge_tiles(tiles):
    top = functools.reduce(jnp.maximum, tiles)
    scales = [jnp.exp2((t - top) * COEF) for t in tiles]
    total = sum(pltpu.roll(e, 64, 1) * t for e, t in zip(scales, tiles))
    lane = lax.broadcasted_iota(jnp.int32, (8, 128), 1)
    return jnp.where(lane < 64, top, total), scales


def pack_tile(tile):
    high = tile.astype(BF16).astype(F32)
    return jnp.concatenate([high, tile - high], 0).astype(BF16)


def unpack_tile(rows):
    rows = rows.astype(F32)
    return rows[:8] + rows[8:]


def scale_rows(scale, rows):
    n = rows.shape[0] // 8
    return jnp.concatenate([lane_bcast(scale, k) * rows[8 * k : 8 * k + 8] for k in range(n)], 0)


def kernel(
    q_hbm, root_hbm, doc_hbm, suf_hbm, new_hbm, len_hbm, rd_hbm, ol_hbm, dr_hbm,
    out_ref,
    qbuf, raw, f32s, keys, vals, suf, newb, newf, tail_s, len_s, rd_s, ol_s, dr_s,
    ns1, nr1, own2, ss2, ns2, nr2, ns3, nr3,
    tail_num, tail_m, tail_l,
    lsem, kvs, kvr, zs, zr, bs, br_, as_, ar_, r1s, r1r, r2s, r2r, r3s, r3r,
):
    me = lax.axis_index("seq")
    core = lax.rem(me, 2)
    z = lax.rem(me // 2, 4)
    y = lax.rem(me // 8, 4)
    x = me // 32

    def dev(xx, yy, zz, cc):
        return {"seq": ((xx * 4 + yy) * 4 + zz) * 2 + cc}

    def zpeer(d, c):
        return dev(x, y, lax.rem(z + d, 4), c)

    def xpeer(d, c):
        return dev(lax.rem(x + d, 4), y, z, c)

    def ypeer(d, c):
        return dev(x, lax.rem(y + d, 4), z, c)

    def along(x_step, y_step, c):
        return dev(lax.rem(x + x_step, 4), lax.rem(y + y_step, 4), z, c)

    apeer = (xpeer, ypeer)
    bpeer = (ypeer, xpeer)
    partner = dev(x, y, z, 1 - core)

    local = []

    def fetch(src, dst):
        c = pltpu.make_async_copy(src, dst, lsem.at[len(local)])
        c.start()
        local.append(c)
        return c

    c_q = fetch(q_hbm, qbuf.at[0, 0, 0, 0])
    c_root = fetch(root_hbm, raw.at[0, 0])
    c_doc = fetch(doc_hbm, raw.at[1, 0])
    c_ol = fetch(ol_hbm, ol_s)
    c_rd = fetch(rd_hbm, rd_s)
    c_dr = fetch(dr_hbm, dr_s)
    c_len = fetch(len_hbm, len_s)
    c_new = fetch(new_hbm, newb)
    c_suf = fetch(suf_hbm, suf)

    barrier = pltpu.get_barrier_semaphore()
    axes = [(f, d) for f in (xpeer, ypeer, zpeer) for d in (1, 2, 3)]
    peers = [partner] + [f(d, c) for f, d in axes for c in (core, 1 - core)]
    for p in peers:
        pl.semaphore_signal(barrier, inc=1, device_id=p, device_id_type=pl.DeviceIdType.MESH)
    pl.semaphore_wait(barrier, len(peers))

    def send(src, dst, ss, rs, to):
        c = pltpu.make_async_remote_copy(
            src_ref=src, dst_ref=dst, send_sem=ss, recv_sem=rs,
            device_id=to, device_id_type=pl.DeviceIdType.MESH,
        )
        c.start()
        return c

    def wait_for(ref, sem):
        pltpu.make_async_copy(ref, ref, sem).wait()

    sent = []

    def to_b(path, zz):
        for d in (3, 2, 1):
            r = 4 - d
            sent.append(send(qbuf.at[path, 0, 0, zz], qbuf.at[path, 0, r, zz], bs.at[path, d - 1, zz], br_.at[path, r - 1, zz], bpeer[path](d, core)))

    def to_a(path, zz):
        for d in (3, 2, 1):
            r = 4 - d
            sent.append(send(qbuf.at[path, 0, 0, zz], qbuf.at[path, r, 0, zz], as_.at[path, d - 1, zz], ar_.at[path, r - 1, zz], apeer[path](d, core)))

    def on_to_a(path, b_rel):
        for d in (3, 2, 1):
            r = 4 - d
            sent.append(send(qbuf.at[path, 0, b_rel], qbuf.at[path, r, b_rel], as_.at[path, d - 1, b_rel + 1], ar_.at[path, r - 1, b_rel + 1], apeer[path](d, core)))

    c_q.wait()
    for d in (3, 2, 1):
        r = 4 - d
        sent.append(send(qbuf.at[0, 0, 0, 0], qbuf.at[r // 2, 0, 0, r % 2], zs.at[d - 1], zr.at[r - 1], zpeer(d, core)))
    to_b(0, 0)
    kv_root = send(root_hbm, raw.at[0, 1], kvs.at[0], kvr.at[0], partner)
    kv_doc = send(doc_hbm, raw.at[1, 1], kvs.at[1], kvr.at[1], partner)

    vals[:, :, HD:] = jnp.ones((2, 1024, HD), BF16)
    newf[...] = jnp.zeros_like(newf)

    def split_heads(src, who):
        for kv in range(2):
            f32s[src, who, kv] = raw[src, who, kv].astype(F32)
            base = src * 512 + who * 256
            for h in range(2):
                part = f32s[src, who, kv, pl.ds(h, 256, stride=2), :].astype(BF16)
                if kv == 0:
                    keys[h, base : base + 256] = part
                else:
                    vals[h, base : base + 256, :HD] = part

    c_root.wait()
    split_heads(0, 0)
    c_doc.wait()
    split_heads(1, 0)

    for r in (1, 3, 2):
        path, zz = r // 2, r % 2
        wait_for(qbuf.at[path, 0, 0, zz], zr.at[r - 1])
        to_b(path, zz)
    for path in range(2):
        for zz in range(2):
            to_a(path, zz)

    kv_root.wait_recv()
    split_heads(0, 1)
    kv_doc.wait_recv()
    split_heads(1, 1)

    for path in range(2):
        for r in (1, 3, 2):
            for zz in range(2):
                wait_for(qbuf.at[path, 0, r, zz], br_.at[path, r - 1, zz])
            on_to_a(path, r)

    for c in (c_ol, c_rd, c_dr, c_len, c_new, c_suf):
        c.wait()
    length = len_s[0]
    qown = qbuf[0, 0, 0, 0]
    row = lax.broadcasted_iota(jnp.int32, (ROWS, 1024), 0)
    col = lax.broadcasted_iota(jnp.int32, (ROWS, 1024), 1)
    same = (row // 8) % 2 == col % 2
    tops = []
    for c in range(4):
        s = lax.dot_general(qown, suf[0, 1024 * c : 1024 * c + 1024], NT, preferred_element_type=F32)
        s = jnp.where(same & (col // 2 < length - 512 * c), s, -BIG)
        tail_s[:, 1024 * c : 1024 * c + 1024] = s
        tops.append(jnp.max(s, 1, keepdims=True))
    for kv in range(2):
        for j in range(3):
            newf[kv, 2 * j : 2 * j + 2] = newb[kv, j].astype(F32)
    s_new = lax.dot_general(qown, newf[0].astype(BF16), NT, preferred_element_type=F32)
    r128, c128 = row[:, :128], col[:, :128]
    s_new = jnp.where(((r128 // 8) % 2 == c128 % 2) & (c128 // 2 <= r128 // 16) & (c128 < 6), s_new, -BIG)
    tops.append(jnp.max(s_new, 1, keepdims=True))
    top = functools.reduce(jnp.maximum, tops)
    p_new = jnp.exp2((s_new - top) * COEF).astype(BF16)
    num = lax.dot_general(p_new, newf[1].astype(BF16), (((1,), (0,)), ((), ())), preferred_element_type=F32)
    total = jnp.sum(p_new.astype(F32), 1, keepdims=True)
    for c in range(4):
        p = jnp.exp2((tail_s[:, 1024 * c : 1024 * c + 1024] - top) * COEF).astype(BF16)
        num += jnp.dot(p, suf[1, 1024 * c : 1024 * c + 1024], preferred_element_type=F32)
        total += jnp.sum(p.astype(F32), 1, keepdims=True)
    tail_num[...] = num
    tail_m[...] = jnp.broadcast_to(top, (ROWS, 128))
    tail_l[...] = jnp.broadcast_to(total, (ROWS, 128))

    lane = lax.broadcasted_iota(jnp.int32, (8, 128), 1)
    chip = me // 2

    def block(a_rel):
        q = qbuf[:, a_rel].reshape(16 * ROWS, HD).astype(F32).reshape(48, 2, 8, HD)
        bars = []
        for path in range(2):
            for b_rel in range(4):
                xx = lax.rem(x + (b_rel if path else a_rel), 4)
                yy = lax.rem(y + (a_rel if path else b_rel), 4)
                for zz in range(2):
                    slot = ((xx * 4 + yy) * 4 + lax.rem(z + 2 * path + zz, 4)) * 2 + core
                    run = dr_s[rd_s[ol_s[slot]]]
                    bars.append(jnp.full((24, 1), jnp.where(run == chip, 0.0, BIG), F32))
        bar = jnp.concatenate(bars, 0)
        nums, tiles = [], [jnp.zeros((8, 128), F32)] * 2
        for h in range(2):
            qh = q[:, h].reshape(48 * 8, HD).astype(BF16)
            s = lax.dot_general(qh, keys[h], NT, preferred_element_type=F32)
            s0, s1 = s[:, :512], s[:, 512:]
            m = jnp.maximum(jnp.max(s0, 1, keepdims=True), jnp.max(s1, 1, keepdims=True) - bar)
            m = m.astype(BF16).astype(F32)
            p0 = jnp.exp2((s0 - m) * COEF).astype(BF16)
            p1 = jnp.exp2((s1 - (m + bar)) * COEF).astype(BF16)
            o = jnp.dot(p0, vals[h, :512], preferred_element_type=F32)
            o += jnp.dot(p1, vals[h, 512:], preferred_element_type=F32)
            nums.append(o[:, :HD].reshape(48, 1, 8, HD))
            for i in range(48):
                k = 2 * (i % 24) + h
                tile = jnp.where(lane == k, m[8 * i : 8 * i + 8], tiles[i // 24])
                tiles[i // 24] = jnp.where(lane == 64 + k, o[8 * i : 8 * i + 8, HD:], tile)
        ns1[:, a_rel, : 8 * ROWS] = jnp.concatenate(nums, 1).reshape(2, 8 * ROWS, HD).astype(BF16)
        for path in range(2):
            ns1[path, a_rel, 8 * ROWS :] = pack_tile(tiles[path])

    def rs1(path, d):
        r = lax.rem(4 - d, 4)
        to = along(jnp.where(path == 0, d, 0), jnp.where(path == 0, 0, d), 1)
        return pltpu.make_async_remote_copy(
            src_ref=ns1.at[path, d], dst_ref=nr1.at[core, path, r], send_sem=r1s.at[path, d],
            recv_sem=r1r.at[core, path, r], device_id=to, device_id_type=pl.DeviceIdType.MESH)

    def step(a_rel, carry):
        @pl.when(a_rel > 0)
        def _():
            for path in range(2):
                for zz in range(2):
                    wait_for(qbuf.at[path, a_rel, 0, zz], ar_.at[path, a_rel - 1, zz])
                for b_rel in range(1, 4):
                    wait_for(qbuf.at[path, a_rel, b_rel], ar_.at[path, a_rel - 1, b_rel + 1])

        block(a_rel)

        @pl.when((a_rel > 0) | (core == 0))
        def _():
            for path in range(2):
                rs1(path, a_rel).start()

        @pl.when((a_rel == 0) & (core == 1))
        def _():
            for path in range(2):
                pltpu.make_async_copy(ns1.at[path, 0], nr1.at[1, path, 0], r1r.at[1, path, 0]).start()

        return carry

    lax.fori_loop(0, 4, step, 0)

    def rs2(plane, path, d):
        r = 4 - d
        to = along(jnp.where(path == 0, 0, d), jnp.where(path == 0, d, 0), 1)
        return pltpu.make_async_remote_copy(
            src_ref=ns2.at[plane, path, d - 1], dst_ref=nr2.at[plane, path, r - 1], send_sem=r2s.at[plane, path, d - 1],
            recv_sem=r2r.at[plane, path, r - 1], device_id=to, device_id_type=pl.DeviceIdType.MESH)

    def rs3(plane, path, zz):
        d = 2 * path + zz
        r = lax.rem(4 - d, 4)
        return pltpu.make_async_remote_copy(
            src_ref=ns3.at[plane, d], dst_ref=nr3.at[r], send_sem=r3s.at[plane, d], recv_sem=r3r.at[r],
            device_id=zpeer(d, plane), device_id_type=pl.DeviceIdType.MESH)

    def back_a(i, carry):
        plane, path = 1 - lax.rem(i, 2), i // 2
        for r in (0, 3, 2, 1):
            wait_for(nr1.at[plane, path, r], r1r.at[plane, path, r])
        msgs = [nr1.at[plane, path, r] for r in range(4)]
        tile, scales = merge_tiles([unpack_tile(p[8 * ROWS :]) for p in msgs])
        acc = sum(scale_rows(e, p[: 8 * ROWS].astype(F32)) for e, p in zip(scales, msgs))
        own2[plane, path] = acc[:96]
        ss2[plane, path] = tile
        for d in (2, 1, 3):
            ns2[plane, path, d - 1, :96] = acc[96 * d : 96 * (d + 1)].astype(BF16)
            ns2[plane, path, d - 1, 96:] = pack_tile(tile)
        for d in (2, 1, 3):
            rs2(plane, path, d).start()
        return carry

    def back_b(i, carry):
        plane, path = 1 - lax.rem(i, 2), i // 2
        for r in (1, 3, 2):
            wait_for(nr2.at[plane, path, r - 1], r2r.at[plane, path, r - 1])
        tiles = [ss2[plane, path]]
        tiles += [pltpu.roll(unpack_tile(nr2[plane, path, r - 1, 96:]), 128 - 12 * (4 - r), 1) for r in (1, 2, 3)]
        tile, scales = merge_tiles(tiles)
        acc = scale_rows(scales[0], own2[plane, path])
        for r in range(3):
            acc += scale_rows(scales[r + 1], nr2[plane, path, r, :96].astype(F32))
        for zz in range(2):
            ns3[plane, 2 * path + zz, :ROWS] = acc[ROWS * zz : ROWS * zz + ROWS].astype(BF16)
            ns3[plane, 2 * path + zz, ROWS:] = pack_tile(tile)
        here = (plane == 1) & (path == 0)

        @pl.when(jnp.logical_not(here))
        def _():
            rs3(plane, path, 0).start()

        @pl.when(here)
        def _():
            pltpu.make_async_copy(ns3.at[1, 0], nr3.at[0], r3r.at[0]).start()

        rs3(plane, path, 1).start()
        return carry

    @pl.when(core == 1)
    def _():
        lax.fori_loop(0, 4, back_a, 0)
        lax.fori_loop(0, 4, back_b, 0)

    for r in (0, 3, 1, 2):
        wait_for(nr3.at[r], r3r.at[r])
    parts = []
    for r in range(4):
        t = unpack_tile(nr3[r, ROWS:])
        parts.append((nr3[r, :ROWS].astype(F32), pltpu.roll(t, 128 - 6, 1) if r % 2 else t))
    for k in range(6):
        at = slice(8 * k, 8 * k + 8)
        tops = [lane_bcast(t, k) for _, t in parts] + [tail_m[at]]
        sums = [lane_bcast(t, 64 + k) for _, t in parts] + [tail_l[at]]
        nums = [n[at] for n, _ in parts] + [tail_num[at]]
        top = functools.reduce(jnp.maximum, tops)
        es = [jnp.exp2((t - top) * COEF) for t in tops]
        den = sum(e * s for e, s in zip(es, sums))
        res = sum(e * v for e, v in zip(es, nums)) / den
        for g in range(8):
            col = (8 * (k % 2) + g) * HD
            out_ref[0, k // 2 : k // 2 + 1, col : col + HD] = res[g : g + 1].astype(BF16)

    kv_root.wait_send()
    kv_doc.wait_send()
    for path in range(2):
        for d in (1, 2, 3):
            wait_for(ns1.at[path, d], r1s.at[path, d])

    for c in sent:
        c.wait_send()

    @pl.when(core == 0)
    def _():
        for path in range(2):
            wait_for(ns1.at[path, 0], r1s.at[path, 0])

    @pl.when(core == 1)
    def _():
        for plane in range(2):
            for path in range(2):
                for d in (1, 2, 3):
                    wait_for(ns2.at[plane, path, d - 1], r2s.at[plane, path, d - 1])
            for d in range(4):
                if (plane, d) != (1, 0):
                    wait_for(ns3.at[plane, d], r3s.at[plane, d])


def body(queries, root_kv, doc_kv, suffix_kv, new_kv, suffix_len, request_doc, owner_list, doc_run):
    vm, dma = pltpu.VMEM, pltpu.SemaphoreType.DMA
    any_spec = pl.BlockSpec(memory_space=pltpu.HBM)
    out = pl.pallas_call(
        kernel,
        out_shape=pltpu.VMEM((1, 3, 2048), BF16),
        in_specs=[any_spec] * 9,
        out_specs=pl.BlockSpec(memory_space=pltpu.VMEM),
        scratch_shapes=[
            vm((2, 4, 4, 2, ROWS, HD), BF16),
            vm((2, 2, 2, 512, HD), BF16),
            vm((2, 2, 2, 512, HD), F32),
            vm((2, 1024, HD), BF16),
            vm((2, 1024, 2 * HD), BF16),
            vm((2, 4096, HD), BF16),
            vm((2, 3, 2, HD), BF16),
            vm((2, 128, HD), F32),
            vm((ROWS, 4096), F32),
            pltpu.SMEM((1,), jnp.int32),
            pltpu.SMEM((128,), jnp.int32),
            pltpu.SMEM((128,), jnp.int32),
            pltpu.SMEM((64,), jnp.int32),
            vm((2, 4, 8 * ROWS + 16, HD), BF16),
            vm((2, 2, 4, 8 * ROWS + 16, HD), BF16),
            vm((2, 2, 96, HD), F32),
            vm((2, 2, 8, 128), F32),
            vm((2, 2, 3, 112, HD), BF16),
            vm((2, 2, 3, 112, HD), BF16),
            vm((2, 4, 64, HD), BF16),
            vm((4, 64, HD), BF16),
            vm((ROWS, HD), F32),
            vm((ROWS, HD), F32),
            vm((ROWS, HD), F32),
            dma((9,)),
            dma((2,)), dma((2,)),
            dma((3,)), dma((3,)),
            dma((2, 3, 2)), dma((2, 3, 2)),
            dma((2, 3, 5)), dma((2, 3, 5)),
            dma((2, 4)), dma((2, 2, 4)),
            dma((2, 2, 3)), dma((2, 2, 3)),
            dma((2, 4)), dma((4,)),
        ],
        compiler_params=pltpu.CompilerParams(
            collective_id=0, has_side_effects=True, vmem_limit_bytes=60 * 1024 * 1024
        ),
    )(
        queries.reshape(ROWS, HD),
        root_kv.reshape(2, 512, HD),
        doc_kv.reshape(2, 512, HD),
        suffix_kv.reshape(2, 4096, HD),
        new_kv.reshape(2, 3, 2, HD),
        suffix_len,
        request_doc.reshape(128),
        owner_list,
        doc_run,
    )
    return out


def solution(mesh):
    in_specs = (
        P("seq", None, "kvh", None, None),
        P(None, "seq", "kvh", None),
        P(None, "seq", "kvh", None),
        P(None, "seq", None, "kvh", None),
        P(None, "seq", None, "kvh", None),
        P("seq"),
        P(),
        P(),
        P(),
    )
    out_specs = P("seq", None, "kvh")
    return jax.shard_map(body, mesh=mesh, in_specs=in_specs, out_specs=out_specs, check_vma=False)
```

time: 40.9 us -> 37.3 us (0.912)
  the two profiles are of different devices: /device:TPU:32 before, /device:TPU:1 now
where the time goes in v3:
time: 37.3 us; the launch traced here: 37.2 us
  Pallas kernels  36 us (97%)
  between operations  0.66 us (2%)
  local copies, waits for them, and re-layouts  0.61 us (2%)
    pallas_call x1, Pallas kernels, body(): pl.pallas_call(kernel, out_shape=pltpu.VMEM((1, 3, 2048), BF16), in_specs...  36 us

profile of v3, /device:TPU:1, one launch (start us, length us, event | category | flops | bytes accessed | tf_op | source)
XLA Modules:
  0.0 37.2 jit_solution(5481198381640264442)
XLA Ops:
  0.7 36.0 %shard_map.91 = bf16[1,3,2048]{2,1,0:T(4,128)(2,1)S(1)} custom-call(bf16[48,128]{1,0:T(8,128)(2,1)} %bitcast.9, bf16[2,512,128]{2,1,0:T(8,128)(2,1)} %bitcast.7, bf16[2,512,128]{2,1,0:T(8,128)(2,1)} %bitcast.8, bf16[2,4096,128]{2,1,0:T(8,128)(2,1)} %bitcast.6, bf16[2,3,2,128]{3,2,1,0:T(2,128)(2,1)} %bitcast.10, s32[1]{0:T(128)S(6)} %copy.12.len_hbm, ...), custom_call_target="tpu_custom_call" | custom-call | tf_op jit(solution)/shard_map/pallas_call | solution.py:386
  36.6 0.6 %copy.11 = bf16[1,3,2048]{2,1,0:T(4,128)(2,1)} copy(bf16[1,3,2048]{2,1,0:T(4,128)(2,1)S(1)} %shard_map.91) | data formatting | bytes 24576

commit v4 on v3

--- a/solution.py
+++ b/solution.py
@@ -120,15 +120,14 @@
             r = 4 - d
             sent.append(send(qbuf.at[path, 0, 0, zz], qbuf.at[path, 0, r, zz], bs.at[path, d - 1, zz], br_.at[path, r - 1, zz], bpeer[path](d, core)))
 
-    def to_a(path, zz):
+    def to_a(path):
         for d in (3, 2, 1):
             r = 4 - d
-            sent.append(send(qbuf.at[path, 0, 0, zz], qbuf.at[path, r, 0, zz], as_.at[path, d - 1, zz], ar_.at[path, r - 1, zz], apeer[path](d, core)))
-
-    def on_to_a(path, b_rel):
-        for d in (3, 2, 1):
-            r = 4 - d
-            sent.append(send(qbuf.at[path, 0, b_rel], qbuf.at[path, r, b_rel], as_.at[path, d - 1, b_rel + 1], ar_.at[path, r - 1, b_rel + 1], apeer[path](d, core)))
+            sent.append(send(qbuf.at[path, 0, 0], qbuf.at[path, r, 0], as_.at[path, d - 1, 0], ar_.at[path, r - 1, 0], apeer[path](d, core)))
+
+    def on_to_a(path, d):
+        r = 4 - d
+        sent.append(send(qbuf.at[path, 0, pl.ds(1, 3)], qbuf.at[path, r, pl.ds(1, 3)], as_.at[path, d - 1, 1], ar_.at[path, r - 1, 1], apeer[path](d, core)))
 
     c_q.wait()
     for d in (3, 2, 1):
@@ -162,19 +161,20 @@
         wait_for(qbuf.at[path, 0, 0, zz], zr.at[r - 1])
         to_b(path, zz)
     for path in range(2):
-        for zz in range(2):
-            to_a(path, zz)
+        to_a(path)
 
     kv_root.wait_recv()
     split_heads(0, 1)
     kv_doc.wait_recv()
     split_heads(1, 1)
 
-    for path in range(2):
-        for r in (1, 3, 2):
-            for zz in range(2):
-                wait_for(qbuf.at[path, 0, r, zz], br_.at[path, r - 1, zz])
-            on_to_a(path, r)
+    for d in (3, 2, 1):
+        for path in range(2):
+            if d == 3:
+                for r in (1, 3, 2):
+                    for zz in range(2):
+                        wait_for(qbuf.at[path, 0, r, zz], br_.at[path, r - 1, zz])
+            on_to_a(path, d)
 
     for c in (c_ol, c_rd, c_dr, c_len, c_new, c_suf):
         c.wait()
@@ -232,8 +232,7 @@
             m = m.astype(BF16).astype(F32)
             p0 = jnp.exp2((s0 - m) * COEF).astype(BF16)
             p1 = jnp.exp2((s1 - (m + bar)) * COEF).astype(BF16)
-            o = jnp.dot(p0, vals[h, :512], preferred_element_type=F32)
-            o += jnp.dot(p1, vals[h, 512:], preferred_element_type=F32)
+            o = jnp.dot(jnp.concatenate([p0, p1], 1), vals[h], preferred_element_type=F32)
             nums.append(o[:, :HD].reshape(48, 1, 8, HD))
             for i in range(48):
                 k = 2 * (i % 24) + h
@@ -254,10 +253,8 @@
         @pl.when(a_rel > 0)
         def _():
             for path in range(2):
-                for zz in range(2):
-                    wait_for(qbuf.at[path, a_rel, 0, zz], ar_.at[path, a_rel - 1, zz])
-                for b_rel in range(1, 4):
-                    wait_for(qbuf.at[path, a_rel, b_rel], ar_.at[path, a_rel - 1, b_rel + 1])
+                wait_for(qbuf.at[path, a_rel, 0], ar_.at[path, a_rel - 1, 0])
+                wait_for(qbuf.at[path, a_rel, pl.ds(1, 3)], ar_.at[path, a_rel - 1, 1])
 
         block(a_rel)
 
@@ -417,7 +414,7 @@
             dma((2,)), dma((2,)),
             dma((3,)), dma((3,)),
             dma((2, 3, 2)), dma((2, 3, 2)),
-            dma((2, 3, 5)), dma((2, 3, 5)),
+            dma((2, 3, 2)), dma((2, 3, 2)),
             dma((2, 4)), dma((2, 2, 4)),
             dma((2, 2, 3)), dma((2, 2, 3)),
             dma((2, 4)), dma((4,)),

time: 37.3 us -> 37 us (level)
  no operation moved by 1% of the time
where the time goes in v4:
time: 37 us; the launch traced here: 36.9 us
  Pallas kernels  35.7 us (96%)
  between operations  0.66 us (2%)
  local copies, waits for them, and re-layouts  0.61 us (2%)
    pallas_call x1, Pallas kernels, body(): pl.pallas_call(kernel, out_shape=pltpu.VMEM((1, 3, 2048), BF16), in_specs...  35.7 us

profile of v4, /device:TPU:1, one launch (start us, length us, event | category | flops | bytes accessed | tf_op | source)
XLA Modules:
  0.0 36.9 jit_solution(4257974602026354443)
XLA Ops:
  0.7 35.7 %shard_map.91 = bf16[1,3,2048]{2,1,0:T(4,128)(2,1)S(1)} custom-call(bf16[48,128]{1,0:T(8,128)(2,1)} %bitcast.9, bf16[2,512,128]{2,1,0:T(8,128)(2,1)} %bitcast.7, bf16[2,512,128]{2,1,0:T(8,128)(2,1)} %bitcast.8, bf16[2,4096,128]{2,1,0:T(8,128)(2,1)} %bitcast.6, bf16[2,3,2,128]{3,2,1,0:T(2,128)(2,1)} %bitcast.10, s32[1]{0:T(128)S(6)} %copy.12.len_hbm, ...), custom_call_target="tpu_custom_call" | custom-call | tf_op jit(solution)/shard_map/pallas_call | solution.py:383
  36.3 0.6 %copy.11 = bf16[1,3,2048]{2,1,0:T(4,128)(2,1)} copy(bf16[1,3,2048]{2,1,0:T(4,128)(2,1)S(1)} %shard_map.91) | data formatting | bytes 24576
